TPU v7x, 32 devices: a whole 2x2x4 slice. The times are simulated.
32 devices in a mesh: freq: 4 (over z), sub: 8 (over y, x, core).
Axes of the slice: x: 2, y: 2, z: 4, core: 2. Of those that a mesh axis runs over, the one named last changes fastest.
Arguments:
- sources: float32 [8, 4, 64, 64, 256], P('freq', None, 'sub'), may hold values from -5 to 5
- slowness: float32 [64, 64, 256], P('sub'), may hold values from 0.6 to 1.6
- freq_index: int32 [8], P('freq'), may hold values from 0 to 15
- coverage: int32 [4, 8, 8], P('freq'), may hold values from 0 to 63, as said below
Outputs:
- precond_gradient: float32 [64, 64, 256], P('sub', 'freq')
- delivered: float32 [4, 8, 8, 16, 256], P('freq', 'sub')
Inputs may be any that keep to these rules, and one draw needn't show every extreme that they name: `coverage`: each list names 8 distinct tiles of its depth band; a list names exactly 2 tiles of each owner it names and none of the others, so at most 2 of any one owner.
All inputs are finite; a program needn't handle non-finite values.
Results may differ from a plain program's by a relative error of at most 0.00002.
Values sent between devices are 32-bit elements; how exact they have to be, the bound alone decides.
No kernel may reach another device: no remote copies, remote signals or barrier semaphores. Data moves between devices by JAX's collectives and lax.ppermute only.
A program may use at most 128 MiB of HBM per device.

v0:
```python
import functools

import jax
import jax.numpy as jnp
from jax import lax
from jax.experimental import pallas as pl
from jax.experimental.pallas import tpu as pltpu
from jax.sharding import PartitionSpec as P

TPD = 8
CAP = 2
HALF = 128


def masks():
    lane = lax.broadcasted_iota(jnp.int32, (8, HALF), 1)
    row = lax.broadcasted_iota(jnp.int32, (8, HALF), 0)
    return lane == 0, lane == HALF - 1, row == 0, row == 7


def turn(real, imag, coef_real, coef_imag):
    return real * coef_real + imag * coef_imag, imag * coef_real - real * coef_imag


def coefficients(store, slow, scale, factor, nk):
    for k in range(nk):
        for h in range(2):
            sigma = scale * slow(h, k)
            diag = 0.875 - sigma
            inverse = factor / (diag * diag + sigma * sigma)
            store(0, h, k, diag * inverse)
            store(1, h, k, sigma * inverse)


def relax(store, force, near, coef, marks, nk, base=None):
    lane_first, lane_last, row_first, row_last = marks

    def across(c, h, k):
        before, middle, after = [None if layer is None else layer(c, h, k) for layer in near]
        parts = [part for part in (before, after) if part is not None]
        if middle is not None:
            parts.append(middle + middle)
        return functools.reduce(lambda total, part: total + part, parts)

    both = [(c, h) for c in range(2) for h in range(2)]
    top = {at: across(*at, 0) for at in both}
    bottom = {at: across(*at, nk - 1) for at in both}
    here = top
    pair = {at: jnp.where(row_first, 0.0, pltpu.roll(bottom[at], 1, 0)) + top[at] for at in both}
    for k in range(nk):
        if k < nk - 2:
            following = {at: across(*at, k + 1) for at in both}
        elif k == nk - 2:
            following = bottom
        else:
            following = {at: jnp.where(row_last, 0.0, pltpu.roll(top[at], 7, 0)) for at in both}
        terms = []
        for c in range(2):
            depth = []
            for h in range(2):
                later = here[c, h] + following[c, h]
                depth.append(pair[c, h] + later)
                pair[c, h] = later
            left, right = depth
            left_up, right_up = pltpu.roll(left, HALF - 1, 1), pltpu.roll(right, HALF - 1, 1)
            left_down, right_down = pltpu.roll(left, 1, 1), pltpu.roll(right, 1, 1)
            left_sides = jnp.where(lane_last, right_up, left_up) + jnp.where(lane_first, 0.0, left_down)
            right_sides = jnp.where(lane_last, 0.0, right_up) + jnp.where(
                lane_first, left_down, right_down
            )
            for h, (middle, ends) in enumerate(((left, left_sides), (right, right_sides))):
                total = ends + (middle + middle)
                if near[1] is not None:
                    total = total - 8.0 * near[1](c, h, k)
                terms.append(total if force is None else force(c, h, k) + total)
        here = following
        for h in range(2):
            planes = turn(terms[h], terms[2 + h], coef(0, h, k), coef(1, h, k))
            for c in range(2):
                store(c, h, k, planes[c] if base is None else base(c, h, k) + planes[c])


def piece_of(ref, lead):
    return lambda c, h, k: ref[lead + (c, h, pl.ds(8 * k, 8), slice(None))]


def row_piece(refs, lead, offset, tail, nk):
    return lambda c, h, k: refs[h][
        lead + (offset + c,) + tail + (pl.ds(k, 8, stride=nk), slice(None))
    ]


def store_to(*places):
    def store(c, h, k, piece):
        for ref, lead in places:
            ref[lead + (c, h, pl.ds(8 * k, 8), slice(None))] = piece

    return store


def start_layer(store, force, coef, nk):
    for k in range(nk):
        for h in range(2):
            planes = turn(force(0, h, k), force(1, h, k), coef(0, h, k), coef(1, h, k))
            for c in range(2):
                store(c, h, k, planes[c])


def products(last, acc, place, weight, first, nk):
    for side in range(2):
        forward, adjoint = [piece_of(last, (side, pair)) for pair in range(2)]
        for h in range(2):
            for k in range(nk):
                fr, fi = forward(0, h, k), forward(1, h, k)
                ar, ai = adjoint(0, h, k), adjoint(1, h, k)
                terms = (weight * (fr * ar - fi * ai), weight * (fr * fr + fi * fi))
                for number, term in enumerate(terms):
                    at = (place, number, side, h, pl.ds(k, 8, stride=nk), slice(None))
                    acc[at] = jnp.where(first, term, acc[at] + term)


def write_out(out, acc, offset):
    bands, _, _, _, depth, _ = out.shape
    for band in range(bands):
        for place in range(acc.shape[0]):
            for number in range(2):
                for side in range(2):
                    for h in range(2):
                        out[band, offset + place, number, side, :, pl.ds(h * HALF, HALF)] = acc[
                            place, number, side, h, pl.ds(band * depth, depth), :
                        ]


def scale_of(freq, group):
    weight = 1.0 + freq[group].astype(jnp.float32) / 16.0
    return weight, 0.12 * weight


def parity():
    return lax.axis_index("sub") % 2


def paired(side):
    index = lax.axis_index("sub")
    there = index > 0 if side == 0 else index < lax.axis_size("sub") - 1
    return jnp.where(there, 1.0 / 64.0, 0.0)


def first_kernel(freq, sources, slowness, to_chip, to_core, raw, slow, coef, sems):
    groups, _, layers, rows = sources.shape[:4]
    nk = rows // 8
    places = (parity() * (layers - 1), (1 - parity()) * (layers - 1))
    copies = []
    for side, own in enumerate(places):
        for h in range(2):
            lanes = pl.ds(h * HALF, HALF)
            pairs = ((slowness.at[own, :, lanes], slow), (sources.at[:, :, own, :, lanes], raw))
            for number, (ref, held) in enumerate(pairs):
                copies.append(
                    pltpu.make_async_copy(ref, held.at[side, h], sems.at[side, h, number])
                )
    for copy in copies:
        copy.start()
    for side, out in enumerate((to_chip, to_core)):
        for copy in copies[4 * side : 4 * side + 4]:
            copy.wait()

        def sigma(h, k):
            return slow[side, h, pl.ds(k, 8, stride=nk), :]

        for h in range(2):
            for k in range(nk):
                out[4 * groups, h, pl.ds(8 * k, 8), :] = sigma(h, k)
        for group in range(groups):
            scale = scale_of(freq, group)[1]
            coefficients(store_to((coef, (side, group))), sigma, scale, 1.0 / 64.0, nk)
            for pair in range(2):
                start_layer(
                    store_from(out, (), 4 * group + 2 * pair),
                    row_piece((raw.at[side, 0], raw.at[side, 1]), (group,), 2 * pair, (), nk),
                    piece_of(coef, (side, group)),
                    nk,
                )


def store_from(ref, lead, offset):
    def store(c, h, k, piece):
        ref[lead + (offset + c, h, pl.ds(8 * k, 8), slice(None))] = piece

    return store


def sent_piece(ref, lead, offset):
    return lambda c, h, k: ref[lead + (offset + c, h, pl.ds(8 * k, 8), slice(None))]


def edge_kernel(freq, _, *refs):
    sides = []
    for side in range(2):
        part = refs[12 * side : 12 * side + 12]
        sides.append([[part[at + 2 * n : at + 2 * n + 2] for n in range(3)] for at in (0, 6)])
    far_chip, far_core, second, coef, one, fields = refs[24:]
    group = pl.program_id(0)
    rows = sides[0][1][0][0].shape[-2]
    nk = rows // 8
    marks = masks()
    scale = scale_of(freq, group)[1]
    chains = [(side, pair) for side in range(2) for pair in range(2)]

    def force(side, pair, at):
        return row_piece(sides[side][0][at], (0,), 2 * pair, (0,), nk)

    for side in range(2):
        for at in range(3):
            slows = sides[side][1][at]
            coefficients(
                store_to((coef, (side, at))),
                lambda h, k, slows=slows: slows[h][0, pl.ds(k, 8, stride=nk), :],
                scale,
                1.0 / 64.0,
                nk,
            )
            for pair in range(2):
                start_layer(
                    store_to((one, (side, pair, at))),
                    force(side, pair, at),
                    piece_of(coef, (side, at)),
                    nk,
                )
    for at in range(2):
        for side, pair in chains:
            near = [piece_of(one, (side, pair, n)) if n >= 0 else None for n in (at - 1, at, at + 1)]
            target = (fields, (side, 0, pair)) if at == 0 else (second, (0, pair, side))
            relax(
                store_to(target), force(side, pair, at), near, piece_of(coef, (side, at)), marks, nk
            )
    for side, pair in chains:
        near = [None, piece_of(fields, (side, 0, pair)), piece_of(second, (0, pair, side))]
        relax(
            store_to((fields, (side, 1, pair))),
            force(side, pair, 0),
            near,
            piece_of(coef, (side, 0)),
            marks,
            nk,
        )
    for out, side in ((far_chip, parity()), (far_core, 1 - parity())):
        for level in range(2):
            for pair in range(2):
                for c in range(2):
                    out[level, 0, 2 * pair + c] = fields[side, level, pair, c]


def inner_kernel(
    freq, src_l, src_r, slow_l, slow_r, second,
    out, two_next, three_near, three_far, coef, one, force, two, three, last, acc,
):
    group = pl.program_id(0)
    groups = pl.num_programs(0)
    layers, rows = src_l.shape[2], src_l.shape[3]
    nk = rows // 8
    marks = masks()
    weight, scale = scale_of(freq, group)
    weight = weight * 4096.0
    sources, slows = (src_l, src_r), (slow_l, slow_r)
    chains = [(side, pair) for side in range(2) for pair in range(2)]

    @pl.loop(0, layers - 2)
    def _(place):
        layer = place + 1
        coefficients(
            store_to((coef, (layer,))),
            lambda h, k: slows[h][layer, pl.ds(k, 8, stride=nk), :],
            scale,
            1.0 / 64.0,
            nk,
        )
        for pair in range(2):
            rows_of = row_piece(sources, (0,), 2 * pair, (layer,), nk)
            keep = store_to((force, (pair, layer)))
            for c in range(2):
                for h in range(2):
                    for k in range(nk):
                        keep(c, h, k, rows_of(c, h, k))
            start_layer(store_to((one, (pair, layer))), rows_of, piece_of(coef, (layer,)), nk)

    def copy_plane(keep, given):
        for c in range(2):
            for h in range(2):
                for k in range(nk):
                    keep(c, h, k, given(c, h, k))

    def layer_at(side, at):
        return at if side == 0 else layers - 1 - at

    def step(target, pair, layer, ref, skip):
        near = [piece_of(ref, (pair, layer + shift - skip)) for shift in (-1, 0, 1)]
        relax(
            store_to(target),
            piece_of(force, (pair, layer)),
            near,
            piece_of(coef, (layer,)),
            marks,
            nk,
        )

    for side, pair in chains:
        copy_plane(
            store_to((two, (pair, layer_at(side, 1)))), piece_of(second, (0, pair, side))
        )

    @pl.loop(0, (layers - 4) // 2)
    def _(turn_at):
        for offset in range(2):
            for pair in range(2):
                layer = 2 + 2 * turn_at + offset
                step((two, (pair, layer)), pair, layer, one, 0)

    @pl.loop(0, (layers - 4) // 2)
    def _(turn_at):
        for offset in range(2):
            for pair in range(2):
                layer = 2 + 2 * turn_at + offset
                step((three, (pair, layer - 2)), pair, layer, two, 0)

    for side, pair in chains:
        step((last, (side, pair)), pair, layers // 2 - 1 + side, three, 2)
        for keep, ref, at in (
            (two_next, two, layer_at(side, 2)),
            (three_near, three, layer_at(side, 2) - 2),
            (three_far, three, layer_at(side, 3) - 2),
        ):
            copy_plane(store_to((keep, (0, pair, side))), piece_of(ref, (pair, at)))
    products(last, acc, 0, weight, group == 0, nk)

    @pl.when(group == groups - 1)
    def _():
        write_out(out, acc, 0)


def middle_kernel(freq, *refs):
    sides = []
    for side in range(2):
        part = refs[12 * side : 12 * side + 12]
        sides.append([[part[at + 2 * n : at + 2 * n + 2] for n in range(3)] for at in (0, 6)])
    core_field, core_slow, chip_field, chip_slow, second, two_next, three_near, three_far = refs[24:32]
    out, base_three, base_next, base_four, factors = refs[32:37]
    force, beyond, one, first_two, first_three, halo, halo_slow, change, last, acc = refs[37:]
    group = pl.program_id(0)
    groups = pl.num_programs(0)
    rows = second.shape[-2]
    nk = rows // 8
    marks = masks()
    weight, scale = scale_of(freq, group)
    weight = weight * 4096.0
    chains = [(side, pair) for side in range(2) for pair in range(2)]
    to_chip, to_core = parity(), 1 - parity()
    halo[to_core] = core_field[...]
    halo[to_chip] = chip_field[...]
    halo_slow[to_core] = core_slow[0]
    halo_slow[to_chip] = chip_slow[0]

    for side in range(2):
        coefficients(
            store_to((beyond, (side,))),
            lambda h, k, side=side: halo_slow[side, h, pl.ds(8 * k, 8), :],
            scale,
            paired(side),
            nk,
        )
        for at in range(3):
            slows = sides[side][1][at]
            coefficients(
                store_to((factors, (0, side, at))),
                lambda h, k, slows=slows: slows[h][0, pl.ds(k, 8, stride=nk), :],
                scale,
                1.0 / 64.0,
                nk,
            )
            for pair in range(2):
                rows_of = row_piece(sides[side][0][at], (0,), 2 * pair, (0,), nk)
                keep = store_to((force, (side, pair, at)))
                for c in range(2):
                    for h in range(2):
                        for k in range(nk):
                            keep(c, h, k, rows_of(c, h, k))
                if at < 2:
                    start_layer(
                        store_to((one, (side, pair, at))),
                        rows_of,
                        piece_of(factors, (0, side, at)),
                        nk,
                    )

    def step(target, side, pair, at, near):
        relax(
            store_to(target),
            piece_of(force, (side, pair, at)),
            near,
            piece_of(factors, (0, side, at)),
            marks,
            nk,
        )

    def held(ref, side, pair):
        return piece_of(ref, (0, pair, side))

    for side, pair in chains:
        near = [sent_piece(halo, (side,), 2 * pair)]
        near += [piece_of(one, (side, pair, at)) for at in range(2)]
        step((first_two, (side, pair)), side, pair, 0, near)
    for side, pair in chains:
        near = [None, None, piece_of(one, (side, pair, 0))]
        relax(store_to((change, (0, side, pair))), None, near, piece_of(beyond, (side,)), marks, nk)
    for side, pair in chains:
        near = [
            piece_of(first_two, (side, pair)),
            held(second, side, pair),
            held(two_next, side, pair),
        ]
        step((first_three, (side, pair)), side, pair, 1, near)
    for side, pair in chains:
        near = [
            None,
            piece_of(change, (0, side, pair)),
            piece_of(first_two, (side, pair)),
        ]
        relax(store_to((change, (1, side, pair))), None, near, piece_of(beyond, (side,)), marks, nk)
    for side, pair in chains:
        three = piece_of(first_three, (side, pair))
        near = [three, held(three_near, side, pair), held(three_far, side, pair)]
        step((last, (side, pair)), side, pair, 2, near)
    products(last, acc, 0, weight, group == 0, nk)
    for side, pair in chains:
        three = piece_of(first_three, (side, pair))
        twos = [piece_of(first_two, (side, pair)), held(second, side, pair)]
        changes = [piece_of(change, (number, side, pair)) for number in range(2)]
        for target, at, near in (
            (base_three, 0, [changes[0], *twos]),
            (base_next, 1, [None, three, held(three_near, side, pair)]),
            (base_four, 0, [changes[1], None, three]),
        ):
            step((target, (0, pair, side)), side, pair, at, near)

    @pl.when(group == groups - 1)
    def _():
        write_out(out, acc, 0)


def write_halves(keep, send, acc, place):
    depth = keep.shape[-2]
    odd = lax.axis_index("freq") % 2
    for out, parity_of in ((keep, odd), (send, 1 - odd)):
        for high in range(2):
            start = pl.multiple_of((2 * high + parity_of) * depth, 8)
            for number in range(2):
                for side in range(2):
                    for h in range(2):
                        out[high, number, side, :, pl.ds(h * HALF, HALF)] = acc[
                            place, number, side, h, pl.ds(start, depth), :
                        ]


def outer_kernel(freq, core, chip, base_three, base_next, base_four, factors, *rest):
    outs, (sent_fields, fresh, last, acc) = rest[:4], rest[4:]
    group = pl.program_id(0)
    groups = pl.num_programs(0)
    rows = base_three.shape[-2]
    nk = rows // 8
    marks = masks()
    weight = scale_of(freq, group)[0] * 4096.0
    chains = [(side, pair) for side in range(2) for pair in range(2)]
    to_chip, to_core = parity(), 1 - parity()
    for number in range(2):
        sent_fields[to_core, number] = core[number, 0]
        sent_fields[to_chip, number] = chip[number, 0]

    def step(target, base, side, pair, at, near):
        relax(
            store_to(target),
            None,
            near,
            piece_of(factors, (0, side, at)),
            marks,
            nk,
            base=piece_of(base, (0, pair, side)),
        )

    for side, pair in chains:
        near = [sent_piece(sent_fields, (side, 0), 2 * pair), None, None]
        step((fresh, (side, pair)), base_three, side, pair, 0, near)
    for side, pair in chains:
        near = [piece_of(fresh, (side, pair)), None, None]
        step((last, (0, side, pair)), base_next, side, pair, 1, near)
    for side, pair in chains:
        near = [sent_piece(sent_fields, (side, 1), 2 * pair), piece_of(fresh, (side, pair)), None]
        step((last, (1, side, pair)), base_four, side, pair, 0, near)
    for place in range(2):
        products(last.at[place], acc, place, weight, group == 0, nk)

    @pl.when(group == groups - 1)
    def _():
        for place in range(2):
            write_halves(*outs[2 * place : 2 * place + 2], acc, place)


def fold_kernel(keep, got, send, own):
    high = lax.axis_index("freq") // 2
    send[...] = keep[1 - high] + got[1 - high]
    own[...] = keep[high] + got[high]


def precond_kernel(pick, *refs):
    chunks, (precond, outgoing) = refs[:-2], refs[-2:]
    layers = precond.shape[0]
    wide = [chunk for chunk in chunks if len(chunk.shape) == 6]
    terms = [
        [functools.partial(lambda chunk, other, at: chunk[other, 0, at[0], at[1]], chunk, other)
         for other in range(chunk.shape[0])]
        for chunk in wide
    ]
    flat = chunks[len(wide) :]
    for place in range(0, len(flat), 2):
        terms.append([lambda at, ref=ref: ref[at[0], at[1]] for ref in flat[place : place + 2]])
    for step, parts in enumerate(terms):
        for side in range(2):
            layer = layers // 2 - 1 - step if side == 0 else layers // 2 + step
            grad, illum = [
                functools.reduce(lambda a, b: a + b, [part((number, side)) for part in parts])
                for number in range(2)
            ]
            precond[layer] = grad / jnp.sqrt(illum + 1.0)

    @pl.loop(0, outgoing.shape[0])
    def _(slot):
        outgoing[slot] = precond[pick[slot]]


def deliver_kernel(slots, incoming, out):
    @pl.loop(0, out.shape[2])
    def _(number):
        out[0, 0, number] = incoming[slots[number]]


def smem():
    return pl.BlockSpec(memory_space=pltpu.SMEM)


def vmem():
    return pl.BlockSpec(memory_space=pltpu.VMEM)


def plane_scratch(*lead, rows):
    return pltpu.VMEM(lead + (2, rows, HALF), jnp.float32)


def compiler_params(mebibytes):
    return pltpu.CompilerParams(vmem_limit_bytes=mebibytes * 1024 * 1024)


def light(size=1000):
    return pl.CostEstimate(flops=1000, bytes_accessed=size, transcendentals=0)


def in_hbm(array):
    return pltpu.with_memory_space_constraint(array, pltpu.HBM)


def hbm(*shape):
    return pltpu.HBM(shape, jnp.float32)


def state(groups, rows):
    return (
        hbm(groups, 2, 2, 2, 2, rows, HALF),
        pl.BlockSpec((1, 2, 2, 2, 2, rows, HALF), lambda g: (g, 0, 0, 0, 0, 0, 0)),
    )


def sent(groups, rows):
    return (
        hbm(2, groups, 4, 2, rows, HALF),
        pl.BlockSpec((2, 1, 4, 2, rows, HALF), lambda g: (0, g, 0, 0, 0, 0)),
    )


def factor_state(groups, rows):
    return (
        hbm(groups, 2, 3, 2, 2, rows, HALF),
        pl.BlockSpec((1, 2, 3, 2, 2, rows, HALF), lambda g: (g, 0, 0, 0, 0, 0, 0)),
    )


def sums(bands, rows, columns, steps=1):
    shape = (bands, steps, 2, 2, rows // bands, columns)
    return hbm(*shape), pl.BlockSpec(shape, lambda g: (0,) * 6)


def halves(bands, rows, columns):
    shape = (bands // 2, 2, 2, rows // bands, columns)
    return hbm(*shape), pl.BlockSpec(shape, lambda g: (0,) * 5)


def fold(keep, got):
    shape = hbm(*keep.shape[1:])
    return pl.pallas_call(
        fold_kernel,
        in_specs=[vmem()] * 2,
        out_specs=[vmem()] * 2,
        out_shape=[shape] * 2,
        compiler_params=compiler_params(8),
        cost_estimate=light(),
        name="fold",
    )(keep, got)


def split(pairs):
    return dict(out_shape=[p[0] for p in pairs], out_specs=[p[1] for p in pairs])


def layer_specs(sources, own):
    rows = sources.shape[3]
    return (
        [pl.BlockSpec((1, 4, 1, rows, HALF), lambda g, h=h: (g, 0, own, 0, h)) for h in range(2)],
        [pl.BlockSpec((1, rows, HALF), lambda g, h=h: (own, 0, h)) for h in range(2)],
    )


def first_edges(freq, sources, slowness):
    groups, _, _, rows, _ = sources.shape
    anywhere = pl.BlockSpec(memory_space=pl.ANY)
    return pl.pallas_call(
        first_kernel,
        in_specs=[smem(), anywhere, anywhere],
        out_specs=[vmem()] * 2,
        out_shape=[hbm(4 * groups + 1, 2, rows, HALF)] * 2,
        scratch_shapes=[
            pltpu.VMEM((2, 2, groups, 4, rows, HALF), jnp.float32),
            plane_scratch(2, rows=rows),
            plane_scratch(2, groups, 2, rows=rows),
            pltpu.SemaphoreType.DMA((2, 2, 2)),
        ],
        compiler_params=compiler_params(8),
        cost_estimate=light(),
        name="first",
    )(freq, in_hbm(sources), in_hbm(slowness))


def edge_layers(sources, slowness):
    layers = sources.shape[2]
    sources, slowness = in_hbm(sources), in_hbm(slowness)
    operands, specs = [], []
    for side in range(2):
        parts = [layer_specs(sources, at if side == 0 else layers - 1 - at) for at in range(3)]
        for what, array in enumerate((sources, slowness)):
            for part in parts:
                operands += [array] * 2
                specs += part[what]
    return operands, specs


def later_edges(freq, sources, slowness, first):
    groups, _, _, rows, _ = sources.shape
    operands, specs = edge_layers(sources, slowness)
    operands = [freq, in_hbm(first)] + operands
    specs = [smem(), pl.BlockSpec(memory_space=pl.ANY)] + specs
    return pl.pallas_call(
        edge_kernel,
        grid=(groups,),
        in_specs=specs,
        **split([sent(groups, rows)] * 2 + [state(groups, rows)]),
        scratch_shapes=[
            plane_scratch(2, 3, 2, rows=rows),
            plane_scratch(2, 2, 3, 2, rows=rows),
            plane_scratch(2, 2, 2, 2, rows=rows),
        ],
        compiler_params=compiler_params(32),
        cost_estimate=light(),
        name="edges",
    )(*operands)


def inner(freq, sources, slowness, second, bands):
    groups, _, layers, rows, columns = sources.shape
    half = [
        pl.BlockSpec((1, 4, layers, rows, HALF), lambda g, h=h: (g, 0, 0, 0, h)) for h in range(2)
    ]
    slow = [pl.BlockSpec((layers, rows, HALF), lambda g, h=h: (0, 0, h)) for h in range(2)]
    sources, slowness = in_hbm(sources), in_hbm(slowness)
    return pl.pallas_call(
        inner_kernel,
        grid=(groups,),
        in_specs=[smem()] + half + slow + [state(groups, rows)[1]],
        **split([sums(bands, rows, columns)] + [state(groups, rows)] * 3),
        scratch_shapes=[
            plane_scratch(layers, 2, rows=rows),
            plane_scratch(2, layers, 2, rows=rows),
            plane_scratch(2, layers, 2, rows=rows),
            plane_scratch(2, layers, 2, rows=rows),
            plane_scratch(2, layers - 4, 2, rows=rows),
            plane_scratch(2, 2, 2, rows=rows),
            plane_scratch(1, 2, 2, rows=rows),
        ],
        compiler_params=compiler_params(40),
        cost_estimate=light(),
        name="inner",
    )(freq, sources, sources, slowness, slowness, in_hbm(second))


def middle(freq, sources, slowness, from_core, from_chip, held, bands):
    groups, _, _, rows, columns = sources.shape
    operands, specs = edge_layers(sources, slowness)
    near = [
        pl.BlockSpec((4, 2, rows, HALF), lambda g: (g, 0, 0, 0)),
        pl.BlockSpec((1, 2, rows, HALF), lambda g: (4 * groups, 0, 0, 0)),
    ]
    return pl.pallas_call(
        middle_kernel,
        grid=(groups,),
        in_specs=[smem()] + specs + near * 2 + [state(groups, rows)[1]] * 4,
        **split(
            [sums(bands, rows, columns)] + [state(groups, rows)] * 3 + [factor_state(groups, rows)]
        ),
        scratch_shapes=[
            plane_scratch(2, 2, 3, 2, rows=rows),
            plane_scratch(2, 2, rows=rows),
            plane_scratch(2, 2, 2, 2, rows=rows),
            plane_scratch(2, 2, 2, rows=rows),
            plane_scratch(2, 2, 2, rows=rows),
            plane_scratch(2, 4, rows=rows),
            plane_scratch(2, rows=rows),
            plane_scratch(2, 2, 2, 2, rows=rows),
            plane_scratch(2, 2, 2, rows=rows),
            plane_scratch(1, 2, 2, rows=rows),
        ],
        compiler_params=compiler_params(40),
        cost_estimate=light(100_000_000),
        name="middle",
    )(
        freq, *operands, from_core, from_core, from_chip, from_chip,
        *[in_hbm(array) for array in held],
    )


def outer(freq, from_core, from_chip, held, bands, rows, columns):
    groups = from_core.shape[1]
    return pl.pallas_call(
        outer_kernel,
        grid=(groups,),
        in_specs=[smem()] + [sent(groups, rows)[1]] * 2 + [state(groups, rows)[1]] * 3
        + [factor_state(groups, rows)[1]],
        **split([halves(bands, rows, columns)] * 4),
        scratch_shapes=[
            plane_scratch(2, 2, 4, rows=rows),
            plane_scratch(2, 2, 2, rows=rows),
            plane_scratch(2, 2, 2, 2, rows=rows),
            plane_scratch(2, 2, 2, rows=rows),
        ],
        compiler_params=compiler_params(32),
        cost_estimate=light(),
        name="outer",
    )(freq, from_core, from_chip, *[in_hbm(array) for array in held])


def route(coverage, own_index):
    lists = coverage[0]
    owner, local = lists // TPD, lists % TPD
    position = jnp.arange(lists.shape[1], dtype=jnp.int32)
    same_owner = owner[:, :, None] == owner[:, None, :]
    earlier = position[None, :] < position[:, None]
    rank = jnp.sum((same_owner & earlier[None]).astype(jnp.int32), axis=2)
    slots = jnp.arange(CAP, dtype=jnp.int32)
    hit = (owner == own_index)[:, :, None] & (rank[:, :, None] == slots[None, None, :])
    pick = jnp.sum(jnp.where(hit, local[:, :, None], 0), axis=1).reshape(-1)
    own_slots = owner * CAP + rank
    return pick, lax.dynamic_index_in_dim(own_slots, own_index, 0, keepdims=False)


def body(sources, slowness, freq_index, coverage):
    groups, _, layers, rows, columns = sources.shape
    bands, members = lax.axis_size("freq"), lax.axis_size("sub")
    own_index = lax.axis_index("sub")
    cores = [(i, i ^ 1) for i in range(members)]
    chips = [(i, i + step) for i in range(members) for step in (2 * (i % 2) - 1,) if 0 <= i + step < members]
    def exchange(to_chip, to_core):
        return lax.ppermute(to_chip, "sub", chips), lax.ppermute(to_core, "sub", cores)

    near = first_edges(freq_index, sources, slowness)
    near_chip, near_core = exchange(*near)
    *edges, second = later_edges(freq_index, sources, slowness, near[0])
    far_chip, far_core = exchange(*edges)
    pick, slots = route(coverage, own_index)

    def spread(chunk):
        return lax.all_to_all(chunk, "freq", split_axis=0, concat_axis=0, tiled=True)

    def spread_next(chunk):
        if chunks:
            chunks[-1], chunk = lax.optimization_barrier((chunks[-1], chunk))
        chunks.append(spread(chunk))

    chunks = []
    chunk, *held = inner(freq_index, sources, slowness, second, bands)
    chunk, near_chip, near_core = lax.optimization_barrier((chunk, near_chip, near_core))
    spread_next(chunk)
    held = [second] + held
    chunk, *held = middle(freq_index, sources, slowness, near_core, near_chip, held, bands)
    spread_next(chunk)
    ends = outer(freq_index, far_core, far_chip, held, bands, rows, columns)
    neighbours = [(i, i ^ 1) for i in range(bands)]
    opposites = [(i, i ^ 2) for i in range(bands)]
    got = [lax.ppermute(send, "freq", neighbours) for send in ends[1::2]]
    chunks[-1], got[0] = lax.optimization_barrier((chunks[-1], got[0]))
    for keep, part in zip(ends[::2], got):
        send, own = fold(keep, part)
        chunks += [own, lax.ppermute(send, "freq", opposites)]
    depth = rows // bands
    precond, outgoing = pl.pallas_call(
        precond_kernel,
        in_specs=[smem()] + [vmem()] * len(chunks),
        out_specs=[vmem()] * 2,
        out_shape=[
            jax.ShapeDtypeStruct((layers, depth, columns), jnp.float32),
            jax.ShapeDtypeStruct((members * CAP, depth, columns), jnp.float32),
        ],
        compiler_params=compiler_params(12),
        name="precond",
    )(pick, *chunks)
    incoming = lax.all_to_all(outgoing, "sub", split_axis=0, concat_axis=0, tiled=True)
    delivered = pl.pallas_call(
        deliver_kernel,
        in_specs=[smem(), vmem()],
        out_specs=vmem(),
        out_shape=jax.ShapeDtypeStruct((1, 1, coverage.shape[2], depth, columns), jnp.float32),
        compiler_params=compiler_params(12),
        name="deliver",
    )(slots, incoming)
    return precond, delivered


def solution(mesh):
    placed = (
        P("freq", None, "sub", None, None),
        P("sub", None, None),
        P("freq"),
        P("freq", None, None),
    )
    return jax.shard_map(
        body,
        mesh=mesh,
        in_specs=placed,
        out_specs=(P("sub", "freq", None), P("freq", "sub", None, None, None)),
        check_vma=False,
    )
```

profile of v0, /device:TPU:0, one launch (start us, length us, event | category | flops | bytes accessed | tf_op | source)
XLA Modules:
  0.0 82.6 jit_solution(15147981191267515992)
XLA Ops:
  0.6 0.0 copy-start.4
  0.6 0.6 copy-done.4
  1.3 0.0 copy-start.5
  1.3 2.9 %first.1 = (f32[9,2,64,128]{3,2,1,0:T(8,128)}, f32[9,2,64,128]{3,2,1,0:T(8,128)}) custom-call(s32[2]{0:T(128)S(1)} %copy-done.4, f32[2,4,8,64,256]{4,3,2,1,0:T(8,128)} %refs_17_.3, f32[8,64,256]{2,1,0:T(8,128)} %refs_23_.3), custom_call_target="tpu_custom_call" | custom-call | flops 1000 | bytes 1000 | tf_op jit(solution)/shard_map/first/pallas_call | solution.py:632
  4.2 0.7 collective-permute-start
  4.9 4.3 %collective-permute-start.1 = (f32[9,2,64,128]{3,2,1,0:T(8,128)}, f32[9,2,64,128]{3,2,1,0:T(8,128)S(1)}, u32[]{:S(2)}, u32[]{:S(2)}) collective-permute-start(f32[9,2,64,128]{3,2,1,0:T(8,128)} %get-tuple-element.36), channel_id=1, source_target_pairs={{0,1},{1,0},{2,3},{3,2},{4,5},{5,4},{6,7},{7,6},{8,9},{9,8},{10,11... | collective-permute-start | bytes 1769480 | tf_op jit(solution)/shard_map/ppermute | solution.py:786
  9.3 0.0 copy-done.5
  9.3 5.8 %edges.1 = (f32[2,2,4,2,64,128]{5,4,3,2,1,0:T(8,128)}, f32[2,2,4,2,64,128]{5,4,3,2,1,0:T(8,128)}, f32[2,2,2,2,2,64,128]{6,5,4,3,2,1,0:T(8,128)}) custom-call(s32[2]{0:T(128)S(1)} %copy-done.5, f32[9,2,64,128]{3,2,1,0:T(8,128)} %get-tuple-element.33._, f32[2,4,8,64,256]{4,3,2,1,0:T(8,128)} %refs_17_.3, f32[2,4,8,64,256]{4,3,2,1,0:T(8,128)} %refs_17_.3, ...), custom_call_target="tpu_custom_call" | custom-call | flops 1000 | bytes 1000 | tf_op jit(solution)/shard_map/edges/pallas_call | solution.py:667
  15.0 0.1 collective-permute-start.2
  15.1 0.7 collective-permute-start.3
  15.9 8.4 %inner.1 = (f32[4,1,2,2,16,256]{5,4,3,2,1,0:T(8,128)}, f32[2,2,2,2,2,64,128]{6,5,4,3,2,1,0:T(8,128)}, f32[2,2,2,2,2,64,128]{6,5,4,3,2,1,0:T(8,128)}, f32[2,2,2,2,2,64,128]{6,5,4,3,2,1,0:T(8,128)}) custom-call(s32[2]{0:T(128)S(1)} %copy-done.5, f32[2,4,8,64,256]{4,3,2,1,0:T(8,128)} %refs_17_.3, f32[2,4,8,64,256]{4,3,2,1,0:T(8,128)} %refs_17_.3, ...), custom_call_target="tpu_custom_call" | custom-call | flops 1000 | bytes 1000 | tf_op jit(solution)/shard_map/inner/pallas_call | solution.py:690
  24.2 0.0 collective-permute-done.refs_26_.refs_27_
  24.3 0.0 collective-permute-done.1.refs_24_.refs_25_
  24.3 4.9 %all-to-all-start = ((f32[4,1,2,2,16,256]{5,4,3,2,1,0:T(8,128)}), f32[4,1,2,2,16,256]{5,4,3,2,1,0:T(8,128)S(1)}, u32[]{:S(2)}, u32[]{:S(2)}) async-start(f32[4,1,2,2,16,256]{5,4,3,2,1,0:T(8,128)} %get-tuple-element.37), calls=%async_computation | async-start | bytes 524288 | tf_op jit(solution)/shard_map/all_to_all | solution.py:795
  29.1 0.0 copy-start.6
  29.1 9.6 %middle.1 = (f32[4,1,2,2,16,256]{5,4,3,2,1,0:T(8,128)}, f32[2,2,2,2,2,64,128]{6,5,4,3,2,1,0:T(8,128)}, f32[2,2,2,2,2,64,128]{6,5,4,3,2,1,0:T(8,128)}, f32[2,2,2,...) custom-call(s32[2]{0:T(128)S(1)} %copy-done.5, f32[2,4,8,64,256]{4,3,2,1,0:T(8,128)} %refs_17_.3, ...), custom_call_target="tpu_custom_call" | custom-call | flops 1000 | bytes 100000000 | tf_op jit(solution)/shard_map/middle/pallas_call | solution.py:717
  38.8 0.0 all-to-all-done.refs_0_
  38.8 5.1 %all-to-all-start.1 = ((f32[4,1,2,2,16,256]{5,4,3,2,1,0:T(8,128)}), f32[4,1,2,2,16,256]{5,4,3,2,1,0:T(8,128)S(1)}, u32[]{:S(2)}, u32[]{:S(2)}) async-start(f32[4,1,2,2,16,256]{5,4,3,2,1,0:T(8,128)} %get-tuple-element.45), calls=%async_computation.1 | async-start | bytes 524288 | tf_op jit(solution)/shard_map/all_to_all | solution.py:795
  43.9 0.0 copy-done.6
  43.9 0.0 collective-permute-done.2.core
  43.9 0.0 collective-permute-done.3.chip
  43.9 4.7 %outer.1 = (f32[2,2,2,16,256]{4,3,2,1,0:T(8,128)}, f32[2,2,2,16,256]{4,3,2,1,0:T(8,128)}, f32[2,2,2,16,256]{4,3,2,1,0:T(8,128)}, f32[2,2,2,16,256]{4,3,2,1,0:T(8,128)}) custom-call(s32[2]{0:T(128)S(1)} %copy-done.5, f32[2,2,4,2,64,128]{5,4,3,2,1,0:T(8,128)S(1)} %collective-permute-done.2.core, f32[2,2,4,2,64,128]{5,4,3,2,1,0:T(8,128)S(1)} %collective-permute-done.3.chip, ...), custom_call_target="tpu_custom_call" | custom-call | flops 1000 | bytes 1000 | tf_op jit(solution)/shard_map/outer/pallas_call | solution.py:747
  48.6 2.0 %collective-permute-start.6 = (f32[2,2,2,16,256]{4,3,2,1,0:T(8,128)}, f32[2,2,2,16,256]{4,3,2,1,0:T(8,128)S(1)}, u32[]{:S(2)}, u32[]{:S(2)}) collective-permute-start(f32[2,2,2,16,256]{4,3,2,1,0:T(8,128)} %get-tuple-element.59), channel_id=1, source_target_pairs={{0,8},{8,0},{16,24},{24,16},{1,9},{9,1},{17,25},{25,17},{2,10},{10... | collective-permute-start | bytes 393224 | tf_op jit(solution)/shard_map/ppermute | solution.py:812
  50.7 0.1 collective-permute-start.4
  50.7 0.3 convert_reduce_fusion
  51.0 4.1 %collective-permute-done.6.got = f32[2,2,2,16,256]{4,3,2,1,0:T(8,128)S(1)} collective-permute-done((f32[2,2,2,16,256]{4,3,2,1,0:T(8,128)}, f32[2,2,2,16,256]{4,3,2,1,0:T(8,128)S(1)}, u32[]{:S(2)}, u32[]{:S(2)}) %collective-permute-start.6) | collective-permute-done | bytes 131104 | tf_op jit(solution)/shard_map/ppermute | solution.py:812
  55.2 0.0 copy-start.1
  55.2 0.9 %copy-done.1 = f32[2,2,2,16,256]{4,3,2,1,0:T(8,128)S(1)} copy-done((f32[2,2,2,16,256]{4,3,2,1,0:T(8,128)S(1)}, f32[2,2,2,16,256]{4,3,2,1,0:T(8,128)}, u32[]{:S(2)}) %copy-start.1) | copy-done | bytes 131096
  56.1 0.7 fold.3
  56.7 2.3 %collective-permute-start.7 = (f32[2,2,16,256]{3,2,1,0:T(8,128)}, f32[2,2,16,256]{3,2,1,0:T(8,128)S(1)}, u32[]{:S(2)}, u32[]{:S(2)}) collective-permute-start(f32[2,2,16,256]{3,2,1,0:T(8,128)} %get-tuple-element.61), channel_id=1, source_target_pairs={{0,16},{8,24},{16,0},{24,8},{1,17},{9,25},{17,1},{25,9},{2,18},{10... | collective-permute-start | bytes 196616 | tf_op jit(solution)/shard_map/ppermute | solution.py:816
  59.1 0.0 collective-permute-done.4.got
  59.1 0.0 all-to-all-done.1.refs_1_
  59.1 0.0 copy-start
  59.1 0.9 %copy-done = f32[2,2,2,16,256]{4,3,2,1,0:T(8,128)S(1)} copy-done((f32[2,2,2,16,256]{4,3,2,1,0:T(8,128)S(1)}, f32[2,2,2,16,256]{4,3,2,1,0:T(8,128)}, u32[]{:S(2)}) %copy-start) | copy-done | bytes 131096
  60.0 0.7 fold.2
  60.6 1.2 %collective-permute-start.5 = (f32[2,2,16,256]{3,2,1,0:T(8,128)}, f32[2,2,16,256]{3,2,1,0:T(8,128)S(1)}, u32[]{:S(2)}, u32[]{:S(2)}) collective-permute-start(f32[2,2,16,256]{3,2,1,0:T(8,128)} %get-tuple-element.57), channel_id=1, source_target_pairs={{0,16},{8,24},{16,0},{24,8},{1,17},{9,25},{17,1},{25,9},{2,18},{10... | collective-permute-start | bytes 196616 | tf_op jit(solution)/shard_map/ppermute | solution.py:816
  61.9 0.1 select_reduce_fusion
  62.0 0.1 copy.6
  62.1 0.1 reshape.107.pick
  62.2 0.0 collective-permute-done.7.refs_5_
  62.2 5.7 %collective-permute-done.5.refs_3_ = f32[2,2,16,256]{3,2,1,0:T(8,128)S(1)} collective-permute-done((f32[2,2,16,256]{3,2,1,0:T(8,128)}, f32[2,2,16,256]{3,2,1,0:T(8,128)S(1)}, u32[]{:S(2)}, u32[]{:S(2)}) %collective-permute-start.5) | collective-permute-done | bytes 65568 | tf_op jit(solution)/shard_map/ppermute | solution.py:816
  67.9 0.0 copy-start.2
  68.0 0.8 %copy-done.2 = f32[2,2,16,256]{3,2,1,0:T(8,128)S(1)} copy-done((f32[2,2,16,256]{3,2,1,0:T(8,128)S(1)}, f32[2,2,16,256]{3,2,1,0:T(8,128)}, u32[]{:S(2)}) %copy-start.2) | copy-done | bytes 65560
  68.8 0.8 %copy-done.3 = f32[2,2,16,256]{3,2,1,0:T(8,128)S(1)} copy-done((f32[2,2,16,256]{3,2,1,0:T(8,128)S(1)}, f32[2,2,16,256]{3,2,1,0:T(8,128)}, u32[]{:S(2)}) %copy-start.3) | copy-done | bytes 65560
  69.6 1.5 %precond.1 = (f32[8,16,256]{2,1,0:T(8,128)}, f32[16,16,256]{2,1,0:T(8,128)}) custom-call(s32[16]{0:T(128)S(1)} %reshape.107.pick, f32[4,1,2,2,16,256]{5,4,3,2,1,0:T(8,128)S(1)} %all-to-all-done.refs_0_, f32[4,1,2,2,16,256]{5,4,3,2,1,0:T(8,128)S(1)} %all-to-all-done.1.refs_1_, f32[2,2,16,256]{3,2,1,0:T(8,128)S(1)} %copy-done.3, ...), custom_call_target="tpu_custom_call" | custom-call | tf_op jit(solution)/shard_map/precond/pallas_call | solution.py:818
  71.1 3.4 %all-to-all-start.2 = ((f32[16,16,256]{2,1,0:T(8,128)}), f32[16,16,256]{2,1,0:T(8,128)S(1)}, u32[]{:S(2)}, u32[]{:S(2)}) async-start(f32[16,16,256]{2,1,0:T(8,128)} %get-tuple-element.63), calls=%async_computation.2 | async-start | bytes 524288 | tf_op jit(solution)/shard_map/all_to_all | solution.py:829
  74.5 6.8 %all-to-all-done.2.incoming = f32[16,16,256]{2,1,0:T(8,128)S(1)} async-done(((f32[16,16,256]{2,1,0:T(8,128)}), f32[16,16,256]{2,1,0:T(8,128)S(1)}, u32[]{:S(2)}, u32[]{:S(2)}) %all-to-all-start.2) | async-done | bytes 262176 | tf_op jit(solution)/shard_map/all_to_all | solution.py:829
  81.4 1.2 %deliver.1 = f32[1,1,8,16,256]{4,3,2,1,0:T(8,128)} custom-call(s32[8]{0:T(128)S(1)} %dynamic-slice_bitcast_fusion.slots, f32[16,16,256]{2,1,0:T(8,128)S(1)} %all-to-all-done.2.incoming), custom_call_target="tpu_custom_call" | custom-call | tf_op jit(solution)/shard_map/deliver/pallas_call | solution.py:830
  (5 shorter events, 0.0 us)
Async XLA Ops:
  0.6 0.7 copy-start.4
  1.3 8.0 %copy-start.5 = (s32[2]{0:T(128)S(1)}, s32[2]{0:T(128)}, u32[]{:S(2)}) copy-start(s32[2]{0:T(128)} %freq.9) | copy-start | bytes 28
  4.2 20.0 %collective-permute-start = (f32[9,2,64,128]{3,2,1,0:T(8,128)}, f32[9,2,64,128]{3,2,1,0:T(8,128)S(1)}, u32[]{:S(2)}, u32[]{:S(2)}) collective-permute-start(f32[9,2,64,128]{3,2,1,0:T(8,128)} %get-tuple-element.33._), channel_id=1, source_target_pairs={{1,2},{2,1},{3,4},{4,3},{5,6},{6,5},{9,10},{10,9},{11,12},{12,11},... | collective-permute-start | bytes 1769480 | tf_op jit(solution)/shard_map/ppermute | solution.py:786
  4.9 19.3 %collective-permute-start.1 = (f32[9,2,64,128]{3,2,1,0:T(8,128)}, f32[9,2,64,128]{3,2,1,0:T(8,128)S(1)}, u32[]{:S(2)}, u32[]{:S(2)}) collective-permute-start(f32[9,2,64,128]{3,2,1,0:T(8,128)} %get-tuple-element.36), channel_id=1, source_target_pairs={{0,1},{1,0},{2,3},{3,2},{4,5},{5,4},{6,7},{7,6},{8,9},{9,8},{10,11... | collective-permute-start | bytes 1769480 | tf_op jit(solution)/shard_map/ppermute | solution.py:786
  15.0 28.9 %collective-permute-start.2 = (f32[2,2,4,2,64,128]{5,4,3,2,1,0:T(8,128)}, f32[2,2,4,2,64,128]{5,4,3,2,1,0:T(8,128)S(1)}, u32[]{:S(2)}, u32[]{:S(2)}) collective-permute-start(f32[2,2,4,2,64,128]{5,4,3,2,1,0:T(8,128)} %get-tuple-element.46), channel_id=1, source_target_pairs={{0,1},{1,0},{2,3},{3,2},{4,5},{5,4},{6,7},{7,6},{8,9},{9,8},{10,11... | collective-permute-start | bytes 3145736 | tf_op jit(solution)/shard_map/ppermute | solution.py:786
  15.1 28.8 %collective-permute-start.3 = (f32[2,2,4,2,64,128]{5,4,3,2,1,0:T(8,128)}, f32[2,2,4,2,64,128]{5,4,3,2,1,0:T(8,128)S(1)}, u32[]{:S(2)}, u32[]{:S(2)}) collective-permute-start(f32[2,2,4,2,64,128]{5,4,3,2,1,0:T(8,128)} %get-tuple-element.47), channel_id=1, source_target_pairs={{1,2},{2,1},{3,4},{4,3},{5,6},{6,5},{9,10},{10,9},{11,12},{12,11},... | collective-permute-start | bytes 3145736 | tf_op jit(solution)/shard_map/ppermute | solution.py:786
  24.3 14.5 %all-to-all-start = ((f32[4,1,2,2,16,256]{5,4,3,2,1,0:T(8,128)}), f32[4,1,2,2,16,256]{5,4,3,2,1,0:T(8,128)S(1)}, u32[]{:S(2)}, u32[]{:S(2)}) async-start(f32[4,1,2,2,16,256]{5,4,3,2,1,0:T(8,128)} %get-tuple-element.37), calls=%async_computation | async-start | bytes 524288 | tf_op jit(solution)/shard_map/all_to_all | solution.py:795
  29.1 14.8 %copy-start.6 = (s32[1,8,8]{2,1,0:T(8,128)S(1)}, s32[1,8,8]{2,1,0:T(8,128)}, u32[]{:S(2)}) copy-start(s32[1,8,8]{2,1,0:T(8,128)} %param.7) | copy-start | bytes 772
  38.8 20.3 %all-to-all-start.1 = ((f32[4,1,2,2,16,256]{5,4,3,2,1,0:T(8,128)}), f32[4,1,2,2,16,256]{5,4,3,2,1,0:T(8,128)S(1)}, u32[]{:S(2)}, u32[]{:S(2)}) async-start(f32[4,1,2,2,16,256]{5,4,3,2,1,0:T(8,128)} %get-tuple-element.45), calls=%async_computation.1 | async-start | bytes 524288 | tf_op jit(solution)/shard_map/all_to_all | solution.py:795
  48.6 6.5 %collective-permute-start.6 = (f32[2,2,2,16,256]{4,3,2,1,0:T(8,128)}, f32[2,2,2,16,256]{4,3,2,1,0:T(8,128)S(1)}, u32[]{:S(2)}, u32[]{:S(2)}) collective-permute-start(f32[2,2,2,16,256]{4,3,2,1,0:T(8,128)} %get-tuple-element.59), channel_id=1, source_target_pairs={{0,8},{8,0},{16,24},{24,16},{1,9},{9,1},{17,25},{25,17},{2,10},{10... | collective-permute-start | bytes 393224 | tf_op jit(solution)/shard_map/ppermute | solution.py:812
  50.7 8.4 %collective-permute-start.4 = (f32[2,2,2,16,256]{4,3,2,1,0:T(8,128)}, f32[2,2,2,16,256]{4,3,2,1,0:T(8,128)S(1)}, u32[]{:S(2)}, u32[]{:S(2)}) collective-permute-start(f32[2,2,2,16,256]{4,3,2,1,0:T(8,128)} %get-tuple-element.52), channel_id=1, source_target_pairs={{0,8},{8,0},{16,24},{24,16},{1,9},{9,1},{17,25},{25,17},{2,10},{10... | collective-permute-start | bytes 393224 | tf_op jit(solution)/shard_map/ppermute | solution.py:812
  55.2 0.9 %copy-start.1 = (f32[2,2,2,16,256]{4,3,2,1,0:T(8,128)S(1)}, f32[2,2,2,16,256]{4,3,2,1,0:T(8,128)}, u32[]{:S(2)}) copy-start(f32[2,2,2,16,256]{4,3,2,1,0:T(8,128)} %get-tuple-element.58.keep) | copy-start | bytes 393220
  56.7 5.5 %collective-permute-start.7 = (f32[2,2,16,256]{3,2,1,0:T(8,128)}, f32[2,2,16,256]{3,2,1,0:T(8,128)S(1)}, u32[]{:S(2)}, u32[]{:S(2)}) collective-permute-start(f32[2,2,16,256]{3,2,1,0:T(8,128)} %get-tuple-element.61), channel_id=1, source_target_pairs={{0,16},{8,24},{16,0},{24,8},{1,17},{9,25},{17,1},{25,9},{2,18},{10... | collective-permute-start | bytes 196616 | tf_op jit(solution)/shard_map/ppermute | solution.py:816
  59.1 0.9 %copy-start = (f32[2,2,2,16,256]{4,3,2,1,0:T(8,128)S(1)}, f32[2,2,2,16,256]{4,3,2,1,0:T(8,128)}, u32[]{:S(2)}) copy-start(f32[2,2,2,16,256]{4,3,2,1,0:T(8,128)} %get-tuple-element.54.keep) | copy-start | bytes 393220
  60.6 7.3 %collective-permute-start.5 = (f32[2,2,16,256]{3,2,1,0:T(8,128)}, f32[2,2,16,256]{3,2,1,0:T(8,128)S(1)}, u32[]{:S(2)}, u32[]{:S(2)}) collective-permute-start(f32[2,2,16,256]{3,2,1,0:T(8,128)} %get-tuple-element.57), channel_id=1, source_target_pairs={{0,16},{8,24},{16,0},{24,8},{1,17},{9,25},{17,1},{25,9},{2,18},{10... | collective-permute-start | bytes 196616 | tf_op jit(solution)/shard_map/ppermute | solution.py:816
  67.9 0.8 %copy-start.2 = (f32[2,2,16,256]{3,2,1,0:T(8,128)S(1)}, f32[2,2,16,256]{3,2,1,0:T(8,128)}, u32[]{:S(2)}) copy-start(f32[2,2,16,256]{3,2,1,0:T(8,128)} %get-tuple-element.60.refs_4_) | copy-start | bytes 196612
  68.8 0.8 %copy-start.3 = (f32[2,2,16,256]{3,2,1,0:T(8,128)S(1)}, f32[2,2,16,256]{3,2,1,0:T(8,128)}, u32[]{:S(2)}) copy-start(f32[2,2,16,256]{3,2,1,0:T(8,128)} %get-tuple-element.56.refs_2_) | copy-start | bytes 196612
  71.1 10.3 %all-to-all-start.2 = ((f32[16,16,256]{2,1,0:T(8,128)}), f32[16,16,256]{2,1,0:T(8,128)S(1)}, u32[]{:S(2)}, u32[]{:S(2)}) async-start(f32[16,16,256]{2,1,0:T(8,128)} %get-tuple-element.63), calls=%async_computation.2 | async-start | bytes 524288 | tf_op jit(solution)/shard_map/all_to_all | solution.py:829
where the time goes:
time: 83.2 us; the launch traced here: 82.6 us
  Pallas kernels  35.4 us (43%)
  starting transfers between devices  24.9 us (30%)
  waiting for transfers between devices  16.7 us (20%)
  local copies, waits for them, and re-layouts  4.32 us (5%)
    all_to_all x2, starting transfers between devices, spread(): lax.all_to_all(chunk, 'freq', split_axis=0, concat_axis=0, tiled=True)  9.99 us
    pallas_call x1, Pallas kernels, middle(): pl.pallas_call(middle_kernel, grid=(groups,), in_specs=[smem()] + specs +...  9.64 us
    pallas_call x1, Pallas kernels, inner(): pl.pallas_call(inner_kernel, grid=(groups,), in_specs=[smem()] + half + s...  8.38 us
    all_to_all x1, waiting for transfers between devices, body(): lax.all_to_all(outgoing, 'sub', split_axis=0, concat_axis=0, tiled=True)  6.84 us
    pallas_call x1, Pallas kernels, later_edges(): pl.pallas_call(edge_kernel, grid=(groups,), in_specs=specs, **split([sent...  5.77 us
    ppermute x2, waiting for transfers between devices, body(): chunks += [own, lax.ppermute(send, 'freq', opposites)]  5.75 us
    pallas_call x1, Pallas kernels, outer(): pl.pallas_call(outer_kernel, grid=(groups,), in_specs=[smem()] + [sent(gr...  4.7 us
    ppermute x2, starting transfers between devices, exchange(): lax.ppermute(to_core, 'sub', cores)  4.44 us
  transfers between devices with their start and end apart: 11, of which 3 were waited for; matrix products, arithmetic and copies ran while one was open for 1% of the time, Pallas kernels for 36%

commit v1 on v0

--- a/solution.py
+++ b/solution.py
@@ -146,7 +146,7 @@
     return jnp.where(there, 1.0 / 64.0, 0.0)
 
 
-def first_kernel(freq, sources, slowness, to_chip, to_core, raw, slow, coef, sems):
+def first_kernel(indices, sources, slowness, to_chip, to_core, raw, slow, coef, freq, sems, sem):
     groups, _, layers, rows = sources.shape[:4]
     nk = rows // 8
     places = (parity() * (layers - 1), (1 - parity()) * (layers - 1))
@@ -159,8 +159,11 @@
                 copies.append(
                     pltpu.make_async_copy(ref, held.at[side, h], sems.at[side, h, number])
                 )
+    load = pltpu.make_async_copy(indices, freq, sem)
+    load.start()
     for copy in copies:
         copy.start()
+    load.wait()
     for side, out in enumerate((to_chip, to_core)):
         for copy in copies[4 * side : 4 * side + 4]:
             copy.wait()
@@ -598,16 +601,17 @@
 
 def halves(bands, rows, columns):
     shape = (bands // 2, 2, 2, rows // bands, columns)
-    return hbm(*shape), pl.BlockSpec(shape, lambda g: (0,) * 5)
+    spec = pl.BlockSpec(shape, lambda g: (0,) * 5)
+    return [(jax.ShapeDtypeStruct(shape, jnp.float32), spec), (hbm(*shape), spec)]
 
 
 def fold(keep, got):
-    shape = hbm(*keep.shape[1:])
+    shape = keep.shape[1:]
     return pl.pallas_call(
         fold_kernel,
         in_specs=[vmem()] * 2,
         out_specs=[vmem()] * 2,
-        out_shape=[shape] * 2,
+        out_shape=[hbm(*shape), jax.ShapeDtypeStruct(shape, jnp.float32)],
         compiler_params=compiler_params(8),
         cost_estimate=light(),
         name="fold",
@@ -631,19 +635,21 @@
     anywhere = pl.BlockSpec(memory_space=pl.ANY)
     return pl.pallas_call(
         first_kernel,
-        in_specs=[smem(), anywhere, anywhere],
+        in_specs=[anywhere] * 3,
         out_specs=[vmem()] * 2,
         out_shape=[hbm(4 * groups + 1, 2, rows, HALF)] * 2,
         scratch_shapes=[
             pltpu.VMEM((2, 2, groups, 4, rows, HALF), jnp.float32),
             plane_scratch(2, rows=rows),
             plane_scratch(2, groups, 2, rows=rows),
+            pltpu.SMEM((groups,), jnp.int32),
             pltpu.SemaphoreType.DMA((2, 2, 2)),
+            pltpu.SemaphoreType.DMA,
         ],
         compiler_params=compiler_params(8),
         cost_estimate=light(),
         name="first",
-    )(freq, in_hbm(sources), in_hbm(slowness))
+    )(in_hbm(freq), in_hbm(sources), in_hbm(slowness))
 
 
 def edge_layers(sources, slowness):
@@ -749,7 +755,7 @@
         grid=(groups,),
         in_specs=[smem()] + [sent(groups, rows)[1]] * 2 + [state(groups, rows)[1]] * 3
         + [factor_state(groups, rows)[1]],
-        **split([halves(bands, rows, columns)] * 4),
+        **split(halves(bands, rows, columns) * 2),
         scratch_shapes=[
             plane_scratch(2, 2, 4, rows=rows),
             plane_scratch(2, 2, 2, rows=rows),

time: 83.2 us -> 79.2 us (0.952)
  local copies, waits for them, and re-layouts: 4.32 us -> 0.18 us
  starting transfers between devices: 24.9 us -> 26.6 us
    unnamed x14 -> x4, local copies, waits for them, and re-layouts: 4.14 us -> 0.01 us
    ppermute x2, waiting for transfers between devices: 5.75 us -> 4.83 us  [body(): chunks += [own, lax.ppermute(send, 'freq', opposites)]]
    ppermute x2, starting transfers between devices: 3.59 us -> 4.49 us  [body(): chunks += [own, lax.ppermute(send, 'freq', opposites)]]
  transfers between devices with their start and end apart: 11 -> 11, of which waited for: 3 -> 3; matrix products, arithmetic and copies ran while one was open for 1% -> 1% of each run, Pallas kernels for 36% -> 38%
where the time goes in v1:
time: 79.2 us; the launch traced here: 78.7 us
  Pallas kernels  34.8 us (44%)
  starting transfers between devices  26.6 us (34%)
  waiting for transfers between devices  15.9 us (20%)
    all_to_all x2, starting transfers between devices, spread(): lax.all_to_all(chunk, 'freq', split_axis=0, concat_axis=0, tiled=True)  9.99 us
    pallas_call x1, Pallas kernels, middle(): pl.pallas_call(middle_kernel, grid=(groups,), in_specs=[smem()] + specs +...  9.71 us
    pallas_call x1, Pallas kernels, inner(): pl.pallas_call(inner_kernel, grid=(groups,), in_specs=[smem()] + half + s...  8.39 us
    all_to_all x1, waiting for transfers between devices, body(): lax.all_to_all(outgoing, 'sub', split_axis=0, concat_axis=0, tiled=True)  6.91 us
    pallas_call x1, Pallas kernels, later_edges(): pl.pallas_call(edge_kernel, grid=(groups,), in_specs=specs, **split([sent...  5.73 us
    ppermute x2, waiting for transfers between devices, body(): chunks += [own, lax.ppermute(send, 'freq', opposites)]  4.83 us
    pallas_call x1, Pallas kernels, outer(): pl.pallas_call(outer_kernel, grid=(groups,), in_specs=[smem()] + [sent(gr...  4.6 us
    ppermute x2, starting transfers between devices, body(): chunks += [own, lax.ppermute(send, 'freq', opposites)]  4.49 us
  transfers between devices with their start and end apart: 11, of which 3 were waited for; matrix products, arithmetic and copies ran while one was open for 1% of the time, Pallas kernels for 38%

profile of v1, /device:TPU:0, one launch (start us, length us, event | category | flops | bytes accessed | tf_op | source)
XLA Modules:
  0.0 78.7 jit_solution(3660557087218547333)
XLA Ops:
  0.6 0.0 copy-start
  0.6 2.4 %first.1 = (f32[9,2,64,128]{3,2,1,0:T(8,128)}, f32[9,2,64,128]{3,2,1,0:T(8,128)}) custom-call(s32[2]{0:T(128)} %freq.7, f32[2,4,8,64,256]{4,3,2,1,0:T(8,128)} %refs_17_.3, f32[8,64,256]{2,1,0:T(8,128)} %refs_23_.3), custom_call_target="tpu_custom_call" | custom-call | flops 1000 | bytes 1000 | tf_op jit(solution)/shard_map/first/pallas_call | solution.py:636
  3.1 0.7 collective-permute-start
  3.8 4.3 %collective-permute-start.1 = (f32[9,2,64,128]{3,2,1,0:T(8,128)}, f32[9,2,64,128]{3,2,1,0:T(8,128)S(1)}, u32[]{:S(2)}, u32[]{:S(2)}) collective-permute-start(f32[9,2,64,128]{3,2,1,0:T(8,128)} %get-tuple-element.36), channel_id=1, source_target_pairs={{0,1},{1,0},{2,3},{3,2},{4,5},{5,4},{6,7},{7,6},{8,9},{9,8},{10,11... | collective-permute-start | bytes 1769480 | tf_op jit(solution)/shard_map/ppermute | solution.py:792
  8.1 0.0 copy-done
  8.1 5.7 %edges.1 = (f32[2,2,4,2,64,128]{5,4,3,2,1,0:T(8,128)}, f32[2,2,4,2,64,128]{5,4,3,2,1,0:T(8,128)}, f32[2,2,2,2,2,64,128]{6,5,4,3,2,1,0:T(8,128)}) custom-call(s32[2]{0:T(128)S(1)} %copy-done, f32[9,2,64,128]{3,2,1,0:T(8,128)} %get-tuple-element.33._, f32[2,4,8,64,256]{4,3,2,1,0:T(8,128)} %refs_17_.3, f32[2,4,8,64,256]{4,3,2,1,0:T(8,128)} %refs_17_.3, ...), custom_call_target="tpu_custom_call" | custom-call | flops 1000 | bytes 1000 | tf_op jit(solution)/shard_map/edges/pallas_call | solution.py:673
  13.8 0.1 collective-permute-start.2
  14.0 0.7 collective-permute-start.3
  14.7 8.4 %inner.1 = (f32[4,1,2,2,16,256]{5,4,3,2,1,0:T(8,128)}, f32[2,2,2,2,2,64,128]{6,5,4,3,2,1,0:T(8,128)}, f32[2,2,2,2,2,64,128]{6,5,4,3,2,1,0:T(8,128)}, f32[2,2,2,2,2,64,128]{6,5,4,3,2,1,0:T(8,128)}) custom-call(s32[2]{0:T(128)S(1)} %copy-done, f32[2,4,8,64,256]{4,3,2,1,0:T(8,128)} %refs_17_.3, f32[2,4,8,64,256]{4,3,2,1,0:T(8,128)} %refs_17_.3, ...), custom_call_target="tpu_custom_call" | custom-call | flops 1000 | bytes 1000 | tf_op jit(solution)/shard_map/inner/pallas_call | solution.py:696
  23.1 0.0 collective-permute-done.refs_26_.refs_27_
  23.1 0.0 collective-permute-done.1.refs_24_.refs_25_
  23.1 4.9 %all-to-all-start = ((f32[4,1,2,2,16,256]{5,4,3,2,1,0:T(8,128)}), f32[4,1,2,2,16,256]{5,4,3,2,1,0:T(8,128)S(1)}, u32[]{:S(2)}, u32[]{:S(2)}) async-start(f32[4,1,2,2,16,256]{5,4,3,2,1,0:T(8,128)} %get-tuple-element.37), calls=%async_computation | async-start | bytes 524288 | tf_op jit(solution)/shard_map/all_to_all | solution.py:801
  28.0 0.0 copy-start.1
  28.0 9.7 %middle.1 = (f32[4,1,2,2,16,256]{5,4,3,2,1,0:T(8,128)}, f32[2,2,2,2,2,64,128]{6,5,4,3,2,1,0:T(8,128)}, f32[2,2,2,2,2,64,128]{6,5,4,3,2,1,0:T(8,128)}, f32[2,2,2,...) custom-call(s32[2]{0:T(128)S(1)} %copy-done, f32[2,4,8,64,256]{4,3,2,1,0:T(8,128)} %refs_17_.3, ...), custom_call_target="tpu_custom_call" | custom-call | flops 1000 | bytes 100000000 | tf_op jit(solution)/shard_map/middle/pallas_call | solution.py:723
  37.7 0.0 all-to-all-done.refs_0_
  37.7 5.1 %all-to-all-start.1 = ((f32[4,1,2,2,16,256]{5,4,3,2,1,0:T(8,128)}), f32[4,1,2,2,16,256]{5,4,3,2,1,0:T(8,128)S(1)}, u32[]{:S(2)}, u32[]{:S(2)}) async-start(f32[4,1,2,2,16,256]{5,4,3,2,1,0:T(8,128)} %get-tuple-element.45), calls=%async_computation.1 | async-start | bytes 524288 | tf_op jit(solution)/shard_map/all_to_all | solution.py:801
  42.8 0.0 copy-done.1
  42.8 0.0 collective-permute-done.2.core
  42.8 0.0 collective-permute-done.3.chip
  42.8 4.6 %outer.1 = (f32[2,2,2,16,256]{4,3,2,1,0:T(8,128)S(1)}, f32[2,2,2,16,256]{4,3,2,1,0:T(8,128)}, f32[2,2,2,16,256]{4,3,2,1,0:T(8,128)S(1)}, f32[2,2,2,16,256]{4,3,2,1,0:T(8,128)}) custom-call(s32[2]{0:T(128)S(1)} %copy-done, f32[2,2,4,2,64,128]{5,4,3,2,1,0:T(8,128)S(1)} %collective-permute-done.2.core, ...), custom_call_target="tpu_custom_call" | custom-call | flops 1000 | bytes 1000 | tf_op jit(solution)/shard_map/outer/pallas_call | solution.py:753
  47.4 2.0 %collective-permute-start.6 = (f32[2,2,2,16,256]{4,3,2,1,0:T(8,128)}, f32[2,2,2,16,256]{4,3,2,1,0:T(8,128)S(1)}, u32[]{:S(2)}, u32[]{:S(2)}) collective-permute-start(f32[2,2,2,16,256]{4,3,2,1,0:T(8,128)} %get-tuple-element.59), channel_id=1, source_target_pairs={{0,8},{8,0},{16,24},{24,16},{1,9},{9,1},{17,25},{25,17},{2,10},{10... | collective-permute-start | bytes 393224 | tf_op jit(solution)/shard_map/ppermute | solution.py:818
  49.5 0.1 collective-permute-start.4
  49.5 0.3 convert_reduce_fusion
  49.8 4.2 %collective-permute-done.6.got = f32[2,2,2,16,256]{4,3,2,1,0:T(8,128)S(1)} collective-permute-done((f32[2,2,2,16,256]{4,3,2,1,0:T(8,128)}, f32[2,2,2,16,256]{4,3,2,1,0:T(8,128)S(1)}, u32[]{:S(2)}, u32[]{:S(2)}) %collective-permute-start.6) | collective-permute-done | bytes 131104 | tf_op jit(solution)/shard_map/ppermute | solution.py:818
  54.0 0.6 fold.3
  54.6 2.3 %collective-permute-start.7 = (f32[2,2,16,256]{3,2,1,0:T(8,128)}, f32[2,2,16,256]{3,2,1,0:T(8,128)S(1)}, u32[]{:S(2)}, u32[]{:S(2)}) collective-permute-start(f32[2,2,16,256]{3,2,1,0:T(8,128)} %get-tuple-element.61), channel_id=1, source_target_pairs={{0,16},{8,24},{16,0},{24,8},{1,17},{9,25},{17,1},{25,9},{2,18},{10... | collective-permute-start | bytes 196616 | tf_op jit(solution)/shard_map/ppermute | solution.py:822
  56.9 0.0 collective-permute-done.4.got
  56.9 0.0 all-to-all-done.1.refs_1_
  56.9 0.6 fold.2
  57.6 2.2 %collective-permute-start.5 = (f32[2,2,16,256]{3,2,1,0:T(8,128)}, f32[2,2,16,256]{3,2,1,0:T(8,128)S(1)}, u32[]{:S(2)}, u32[]{:S(2)}) collective-permute-start(f32[2,2,16,256]{3,2,1,0:T(8,128)} %get-tuple-element.57), channel_id=1, source_target_pairs={{0,16},{8,24},{16,0},{24,8},{1,17},{9,25},{17,1},{25,9},{2,18},{10... | collective-permute-start | bytes 196616 | tf_op jit(solution)/shard_map/ppermute | solution.py:822
  59.7 0.1 select_reduce_fusion
  59.9 0.1 copy.6
  60.0 0.1 reshape.107.pick
  60.0 0.0 collective-permute-done.7.refs_5_
  60.1 4.8 %collective-permute-done.5.refs_3_ = f32[2,2,16,256]{3,2,1,0:T(8,128)S(1)} collective-permute-done((f32[2,2,16,256]{3,2,1,0:T(8,128)}, f32[2,2,16,256]{3,2,1,0:T(8,128)S(1)}, u32[]{:S(2)}, u32[]{:S(2)}) %collective-permute-start.5) | collective-permute-done | bytes 65568 | tf_op jit(solution)/shard_map/ppermute | solution.py:822
  64.9 1.4 %precond.1 = (f32[8,16,256]{2,1,0:T(8,128)}, f32[16,16,256]{2,1,0:T(8,128)}) custom-call(s32[16]{0:T(128)S(1)} %reshape.107.pick, f32[4,1,2,2,16,256]{5,4,3,2,1,0:T(8,128)S(1)} %all-to-all-done.refs_0_, f32[4,1,2,2,16,256]{5,4,3,2,1,0:T(8,128)S(1)} %all-to-all-done.1.refs_1_, f32[2,2,16,256]{3,2,1,0:T(8,128)S(1)} %get-tuple-element.56.refs_2_, ...), custom_call_target="tpu_custom_call" | custom-call | tf_op jit(solution)/shard_map/precond/pallas_call | solution.py:824
  66.3 4.2 %all-to-all-start.2 = ((f32[16,16,256]{2,1,0:T(8,128)}), f32[16,16,256]{2,1,0:T(8,128)S(1)}, u32[]{:S(2)}, u32[]{:S(2)}) async-start(f32[16,16,256]{2,1,0:T(8,128)} %get-tuple-element.63), calls=%async_computation.2 | async-start | bytes 524288 | tf_op jit(solution)/shard_map/all_to_all | solution.py:835
  70.6 6.9 %all-to-all-done.2.incoming = f32[16,16,256]{2,1,0:T(8,128)S(1)} async-done(((f32[16,16,256]{2,1,0:T(8,128)}), f32[16,16,256]{2,1,0:T(8,128)S(1)}, u32[]{:S(2)}, u32[]{:S(2)}) %all-to-all-start.2) | async-done | bytes 262176 | tf_op jit(solution)/shard_map/all_to_all | solution.py:835
  77.5 1.2 %deliver.1 = f32[1,1,8,16,256]{4,3,2,1,0:T(8,128)} custom-call(s32[8]{0:T(128)S(1)} %dynamic-slice_bitcast_fusion.slots, f32[16,16,256]{2,1,0:T(8,128)S(1)} %all-to-all-done.2.incoming), custom_call_target="tpu_custom_call" | custom-call | tf_op jit(solution)/shard_map/deliver/pallas_call | solution.py:836
  (4 shorter events, 0.0 us)
Async XLA Ops:
  0.6 7.5 %copy-start = (s32[2]{0:T(128)S(1)}, s32[2]{0:T(128)}, u32[]{:S(2)}) copy-start(s32[2]{0:T(128)} %freq.7) | copy-start | bytes 28
  3.1 20.0 %collective-permute-start = (f32[9,2,64,128]{3,2,1,0:T(8,128)}, f32[9,2,64,128]{3,2,1,0:T(8,128)S(1)}, u32[]{:S(2)}, u32[]{:S(2)}) collective-permute-start(f32[9,2,64,128]{3,2,1,0:T(8,128)} %get-tuple-element.33._), channel_id=1, source_target_pairs={{1,2},{2,1},{3,4},{4,3},{5,6},{6,5},{9,10},{10,9},{11,12},{12,11},... | collective-permute-start | bytes 1769480 | tf_op jit(solution)/shard_map/ppermute | solution.py:792
  3.8 19.3 %collective-permute-start.1 = (f32[9,2,64,128]{3,2,1,0:T(8,128)}, f32[9,2,64,128]{3,2,1,0:T(8,128)S(1)}, u32[]{:S(2)}, u32[]{:S(2)}) collective-permute-start(f32[9,2,64,128]{3,2,1,0:T(8,128)} %get-tuple-element.36), channel_id=1, source_target_pairs={{0,1},{1,0},{2,3},{3,2},{4,5},{5,4},{6,7},{7,6},{8,9},{9,8},{10,11... | collective-permute-start | bytes 1769480 | tf_op jit(solution)/shard_map/ppermute | solution.py:792
  13.8 29.0 %collective-permute-start.2 = (f32[2,2,4,2,64,128]{5,4,3,2,1,0:T(8,128)}, f32[2,2,4,2,64,128]{5,4,3,2,1,0:T(8,128)S(1)}, u32[]{:S(2)}, u32[]{:S(2)}) collective-permute-start(f32[2,2,4,2,64,128]{5,4,3,2,1,0:T(8,128)} %get-tuple-element.46), channel_id=1, source_target_pairs={{0,1},{1,0},{2,3},{3,2},{4,5},{5,4},{6,7},{7,6},{8,9},{9,8},{10,11... | collective-permute-start | bytes 3145736 | tf_op jit(solution)/shard_map/ppermute | solution.py:792
  14.0 28.9 %collective-permute-start.3 = (f32[2,2,4,2,64,128]{5,4,3,2,1,0:T(8,128)}, f32[2,2,4,2,64,128]{5,4,3,2,1,0:T(8,128)S(1)}, u32[]{:S(2)}, u32[]{:S(2)}) collective-permute-start(f32[2,2,4,2,64,128]{5,4,3,2,1,0:T(8,128)} %get-tuple-element.47), channel_id=1, source_target_pairs={{1,2},{2,1},{3,4},{4,3},{5,6},{6,5},{9,10},{10,9},{11,12},{12,11},... | collective-permute-start | bytes 3145736 | tf_op jit(solution)/shard_map/ppermute | solution.py:792
  23.1 14.6 %all-to-all-start = ((f32[4,1,2,2,16,256]{5,4,3,2,1,0:T(8,128)}), f32[4,1,2,2,16,256]{5,4,3,2,1,0:T(8,128)S(1)}, u32[]{:S(2)}, u32[]{:S(2)}) async-start(f32[4,1,2,2,16,256]{5,4,3,2,1,0:T(8,128)} %get-tuple-element.37), calls=%async_computation | async-start | bytes 524288 | tf_op jit(solution)/shard_map/all_to_all | solution.py:801
  28.0 14.8 %copy-start.1 = (s32[1,8,8]{2,1,0:T(8,128)S(1)}, s32[1,8,8]{2,1,0:T(8,128)}, u32[]{:S(2)}) copy-start(s32[1,8,8]{2,1,0:T(8,128)} %param.7) | copy-start | bytes 772
  37.7 19.2 %all-to-all-start.1 = ((f32[4,1,2,2,16,256]{5,4,3,2,1,0:T(8,128)}), f32[4,1,2,2,16,256]{5,4,3,2,1,0:T(8,128)S(1)}, u32[]{:S(2)}, u32[]{:S(2)}) async-start(f32[4,1,2,2,16,256]{5,4,3,2,1,0:T(8,128)} %get-tuple-element.45), calls=%async_computation.1 | async-start | bytes 524288 | tf_op jit(solution)/shard_map/all_to_all | solution.py:801
  47.4 6.5 %collective-permute-start.6 = (f32[2,2,2,16,256]{4,3,2,1,0:T(8,128)}, f32[2,2,2,16,256]{4,3,2,1,0:T(8,128)S(1)}, u32[]{:S(2)}, u32[]{:S(2)}) collective-permute-start(f32[2,2,2,16,256]{4,3,2,1,0:T(8,128)} %get-tuple-element.59), channel_id=1, source_target_pairs={{0,8},{8,0},{16,24},{24,16},{1,9},{9,1},{17,25},{25,17},{2,10},{10... | collective-permute-start | bytes 393224 | tf_op jit(solution)/shard_map/ppermute | solution.py:818
  49.5 7.5 %collective-permute-start.4 = (f32[2,2,2,16,256]{4,3,2,1,0:T(8,128)}, f32[2,2,2,16,256]{4,3,2,1,0:T(8,128)S(1)}, u32[]{:S(2)}, u32[]{:S(2)}) collective-permute-start(f32[2,2,2,16,256]{4,3,2,1,0:T(8,128)} %get-tuple-element.52), channel_id=1, source_target_pairs={{0,8},{8,0},{16,24},{24,16},{1,9},{9,1},{17,25},{25,17},{2,10},{10... | collective-permute-start | bytes 393224 | tf_op jit(solution)/shard_map/ppermute | solution.py:818
  54.6 5.5 %collective-permute-start.7 = (f32[2,2,16,256]{3,2,1,0:T(8,128)}, f32[2,2,16,256]{3,2,1,0:T(8,128)S(1)}, u32[]{:S(2)}, u32[]{:S(2)}) collective-permute-start(f32[2,2,16,256]{3,2,1,0:T(8,128)} %get-tuple-element.61), channel_id=1, source_target_pairs={{0,16},{8,24},{16,0},{24,8},{1,17},{9,25},{17,1},{25,9},{2,18},{10... | collective-permute-start | bytes 196616 | tf_op jit(solution)/shard_map/ppermute | solution.py:822
  57.6 7.3 %collective-permute-start.5 = (f32[2,2,16,256]{3,2,1,0:T(8,128)}, f32[2,2,16,256]{3,2,1,0:T(8,128)S(1)}, u32[]{:S(2)}, u32[]{:S(2)}) collective-permute-start(f32[2,2,16,256]{3,2,1,0:T(8,128)} %get-tuple-element.57), channel_id=1, source_target_pairs={{0,16},{8,24},{16,0},{24,8},{1,17},{9,25},{17,1},{25,9},{2,18},{10... | collective-permute-start | bytes 196616 | tf_op jit(solution)/shard_map/ppermute | solution.py:822
  66.3 11.2 %all-to-all-start.2 = ((f32[16,16,256]{2,1,0:T(8,128)}), f32[16,16,256]{2,1,0:T(8,128)S(1)}, u32[]{:S(2)}, u32[]{:S(2)}) async-start(f32[16,16,256]{2,1,0:T(8,128)} %get-tuple-element.63), calls=%async_computation.2 | async-start | bytes 524288 | tf_op jit(solution)/shard_map/all_to_all | solution.py:835
